TPU v7x, 32 devices: a whole 2x2x4 slice. The times are simulated.
32 devices in a mesh: groups: 2 (over y), blk: 4 (over z), plane: 4 (over x, core).
Axes of the slice: x: 2, y: 2, z: 4, core: 2. Of those that a mesh axis runs over, the one named last changes fastest.
Arguments:
- orbitals: float32 [512, 1, 25600], P(('groups', 'blk'), None, 'plane'), parts along dimension 0, may hold values from -6 to 6
- kernel_half: float32 [1, 81, 81], replicated, may hold values from 0.1 to 10
- pair_own: int32 [384], P(('groups', 'blk')), parts along dimension 0, may hold values from 0 to 63
- pair_step: int32 [384], P(('groups', 'blk')), parts along dimension 0, may hold values from 0 to 2
- pair_remote: int32 [384], P(('groups', 'blk')), parts along dimension 0, may hold values from 0 to 63
- pair_count: int32 [8], P(('groups', 'blk')), parts along dimension 0, may hold values from 6 to 48, as said below
Outputs:
- exchange_part: float32 [512, 1, 25600], P(('groups', 'blk'), None, 'plane'), parts along dimension 0
There are 2 independent parts, one for each index of `groups`. A program takes and returns all parts, laid end to end along the dimension named above; an argument that names none is the same for every part. Nothing has to cross between parts.
Inputs may be any that keep to these rules, and one draw needn't show every extreme that they name: `pair_count`: slots at or beyond a block's count are ignored whatever they hold; in every draw some block has all 48 slots live.
All inputs are finite; a program needn't handle non-finite values.
Results may differ from a plain program's by a relative error of at most 0.0003.
Values sent between devices are 32-bit elements; how exact they have to be, the bound alone decides.
No kernel may reach another device: no remote copies, remote signals or barrier semaphores. Data moves between devices by JAX's collectives and lax.ppermute only.
A program may use at most 64 MiB of HBM per device.

v0:
```python
import functools

import jax
import jax.numpy as jnp
import ml_dtypes
import numpy as np
from jax import lax
from jax.experimental import pallas as pl
from jax.experimental.pallas import tpu as pltpu
from jax.sharding import PartitionSpec as P

NG = 160
STEPS = 3
LANES = 128
GROUP = 4
LINES = 5
FIRST = 8
TOTALS = (17, 19, 21, 24)
EARLY = (6,)
LATE = (3, 3)

VMEM_LIMIT = 16 * 1024 * 1024
highest = lax.Precision.HIGHEST
smem = pl.BlockSpec(memory_space=pltpu.SMEM)
vmem = pl.BlockSpec(memory_space=pltpu.VMEM)
hbm = pl.BlockSpec(memory_space=pl.ANY)


def split_table(table):
    high = table.astype(ml_dtypes.bfloat16)
    low = (table - high.astype(np.float64)).astype(ml_dtypes.bfloat16)
    return high, low


def make_tables(x_local):
    positions = np.arange(NG)
    angles = 2.0 * np.pi / NG * (positions[:, None] * positions[None, :] % NG)
    cas = np.cos(angles) + np.sin(angles)
    into = np.zeros((GROUP, 2 * LANES, NG))
    for r in range(GROUP):
        start = r * NG - r * LANES
        into[r, start : start + NG] = cas
    back = np.transpose(into, (0, 2, 1)).copy()
    order = np.arange(NG).reshape(NG // GROUP, GROUP).T.reshape(-1)
    mixed = cas[:, order]
    return split_table(into), split_table(back), split_table(mixed), split_table(mixed.T.copy())


def split_value(value):
    high = value.astype(jnp.bfloat16)
    low = (value - high.astype(jnp.float32)).astype(jnp.bfloat16)
    return high, low


def dot(a, b):
    return lax.dot_general(a, b, (((1,), (0,)), ((), ())), preferred_element_type=jnp.float32)


def dot3(a, b):
    return dot(a[0], b[0]) + (dot(a[0], b[1]) + dot(a[1], b[0]))


def is_ring(blocks):
    return blocks == STEPS + 1


def route(shift, blocks):
    return [(i, (i + shift) % blocks) for i in range(blocks)]


def plan_kernel(slots, orbs, late, own, step, remote, count, *refs):
    requests, (known, seen, hist) = refs[:STEPS], refs[STEPS:]
    for s in range(STEPS):
        for k in range(slots):
            requests[s][k] = 0
    for s in range(STEPS):
        hist[slots + s] = 0
        for k in range(orbs):
            seen[s * orbs + k] = -1
    for k in range(slots):
        hist[k] = 0

    def visit(j, carry):
        live = j < count[0]
        s = jnp.where(live, step[j], 0)
        k = remote[j]
        at = seen[s * orbs + k]
        used = hist[slots + s]
        rank = jnp.where(at < 0, used, at)

        @pl.when(live & (at < 0))
        def _():
            for i in range(STEPS):

                @pl.when(s == i)
                def _():
                    requests[i][used] = k

            seen[s * orbs + k] = used
            hist[slots + s] = used + 1

        @pl.when(live)
        def _():
            hist[rank] += 1

        known[j] = s
        known[slots + j] = jnp.where(live, rank, 0)
        known[2 * slots + j] = jnp.where(live, own[j], -1)
        return carry

    lax.fori_loop(0, slots, visit, 0)
    beyond = [jnp.int32(0)]
    for k in reversed(range(slots)):
        beyond.append(beyond[-1] + hist[k])
    beyond = beyond[::-1]
    fits = (beyond[FIRST] <= late) & (beyond[TOTALS[-1]] == 0)
    least = sum((beyond[total] > 0).astype(jnp.int32) for total in TOTALS[:-1])
    for s in range(STEPS):
        requests[s][slots] = jnp.where(fits, least, len(TOTALS))


def expand_kernel(half, full):
    rows, columns = full.shape[0], half.shape[1]
    place = lax.broadcasted_iota(jnp.int32, (rows, columns), 0)
    folded = jnp.minimum(place, rows - place)
    picker = (folded == lax.broadcasted_iota(jnp.int32, (rows, columns), 1)).astype(jnp.float32)
    tall = lax.dot_general(
        picker,
        half[0],
        (((1,), (0,)), ((), ())),
        precision=highest,
        preferred_element_type=jnp.float32,
    )
    full[...] = lax.dot_general(
        tall,
        picker,
        (((1,), (1,)), ((), ())),
        precision=highest,
        preferred_element_type=jnp.float32,
    ) * (1.0 / (NG * NG))


def place_kernel(slots, planes, shares, known, *refs):
    place, choice, order, start = refs[-4:]
    largest = refs[0][slots]
    for s in range(1, STEPS + 1):
        largest = jnp.maximum(largest, refs[s][slots])
    choice[0] = largest
    start[0] = 0

    def tally(j, count):
        return count + (known[slots + j] < FIRST).astype(jnp.int32)

    def visit(j, carry):
        chunk = (known[slots + j] >= FIRST).astype(jnp.int32)
        at = start[chunk]
        start[chunk] = at + 1
        order[at] = j
        return carry

    start[1] = lax.fori_loop(0, slots, tally, jnp.int32(0))
    lax.fori_loop(0, slots, visit, 0)
    me = lax.axis_index("plane")
    base = 0
    for size in shares:
        each = size // planes
        for k in range(planes):
            first = base + partner(me, k, planes) * each
            for q in range(each):
                j = order[first + q]
                to = base + k * each + q
                for part in range(3):
                    place[part * slots + to] = known[part * slots + j]
        base += size


def pack_kernel(lines, low, high, wanted, orbitals, sent):
    for c in range(low, high):
        row = wanted[c] * lines
        sent[pl.ds((c - low) * lines, lines), :] = orbitals[pl.ds(row, lines), :]


def packs_kernel(lines, *refs):
    wanted, orbitals, sent = refs[:STEPS], refs[STEPS], refs[STEPS + 1 :]
    for s in range(STEPS):
        for c in range(FIRST, TOTALS[-1]):
            row = orbitals[pl.ds(wanted[s][c] * lines, lines), :]
            for i, total in enumerate(TOTALS):
                if c < total:
                    sent[i * STEPS + s][pl.ds((c - FIRST) * lines, lines), :] = row


def own_kernel(slots, lines, base, size, place, orbitals, owned):
    for j in range(size):
        near = jnp.maximum(place[2 * slots + base + j], 0) * lines
        owned[pl.ds(j * lines, lines), :] = orbitals[pl.ds(near, lines), :]


def density_kernel(slots, lines, planes, bounds, base, size, place, owned, *refs):
    received, parts, kept = refs[: STEPS * len(bounds)], refs[-planes - 1 : -1], refs[-1]
    each = size // planes
    for j in range(size):
        s, rank = place[base + j], place[slots + base + j]
        for c, (low, high) in enumerate(zip((0,) + bounds, bounds)):
            row = jnp.clip(rank - low, 0, high - low - 1) * lines
            found = received[c * STEPS][pl.ds(row, lines), :]
            for i in range(1, STEPS):
                found = jnp.where(s == i, received[c * STEPS + i][pl.ds(row, lines), :], found)
            value = found if c == 0 else jnp.where(rank >= low, found, value)
        kept[pl.ds(j * lines, lines), :] = value
        parts[j // each][pl.ds(j % each * lines, lines), :] = (
            owned[pl.ds(j * lines, lines), :] * value
        )


def sum_kernel(slots, lines, planes, base, size, fresh, place, *refs):
    kept, parts = refs[0], refs[1 : 1 + planes]
    out = refs[-1]
    if fresh:
        out[...] = jnp.zeros_like(out)
    else:
        out[...] = refs[1 + planes][...]
    each = size // planes
    for j in range(size):
        near = place[2 * slots + base + j] * lines

        @pl.when(near >= 0)
        def _():
            out[pl.ds(near, lines), :] += (
                parts[j // each][pl.ds(j % each * lines, lines), :]
                * kept[pl.ds(j * lines, lines), :]
            )


def transform_kernel(pairs, lines, planes, *refs):
    parts = refs[:planes]
    into_hi, into_lo, back_hi, back_lo, mix_hi, mix_lo, unmix_hi, unmix_lo, kernel = refs[
        planes : planes + 9
    ]
    outs = refs[planes + 9 : 2 * planes + 9]
    cells, waves, result = refs[2 * planes + 9 :]
    whole = planes * lines
    rows = NG // GROUP
    me = lax.axis_index("plane")
    for k in range(planes):
        slab = partner(me, k, planes) * lines
        for p in range(pairs):
            cells[pl.ds(p * whole + slab, lines), :] = parts[k][pl.ds(p * lines, lines), :]
    line = [split_value(cells[pl.ds(t, pairs * rows, stride=LINES), :]) for t in range(LINES)]
    for r in range(GROUP):
        wide = [jnp.concatenate([line[r][i], line[r + 1][i]], axis=1) for i in range(2)]
        found = dot3(wide, (into_hi[r], into_lo[r]))
        for p in range(pairs):
            waves[p, r * rows : (r + 1) * rows, :] = found[p * rows : (p + 1) * rows, :]
    mix = (mix_hi[...], mix_lo[...])
    unmix = (unmix_hi[...], unmix_lo[...])
    together = 3 if pairs % 3 == 0 else 1

    def filter_some(i, carry):
        for p in range(together):
            at = i * together + p
            spectrum = dot3(mix, split_value(waves[at])) * kernel[...]
            waves[at] = dot3(unmix, split_value(spectrum))
        return carry

    lax.fori_loop(0, pairs // together, filter_some, 0)
    carried = None
    for r in range(GROUP):
        mine = jnp.concatenate(
            [waves[p, r * rows : (r + 1) * rows, :] for p in range(pairs)], axis=0
        )
        wide = dot3(split_value(mine), (back_hi[r], back_lo[r]))
        first = wide[:, :LANES] if carried is None else wide[:, :LANES] + carried
        carried = wide[:, LANES:]
        result[pl.ds(r, pairs * rows, stride=LINES), :] = first
    result[pl.ds(GROUP, pairs * rows, stride=LINES), :] = carried
    for k in range(planes):
        slab = partner(me, k, planes) * lines
        for p in range(pairs):
            outs[k][pl.ds(p * lines, lines), :] = result[pl.ds(p * whole + slab, lines), :]


def shares_for(slots, planes):
    shares = EARLY + LATE
    units = slots // planes
    cuts = [units * sum(shares[: i + 1]) // sum(shares) for i in range(len(shares))]
    sizes = [(b - a) * planes for a, b in zip([0] + cuts, cuts)]
    return sizes, sum(sizes[len(EARLY) :])


def params():
    return pltpu.CompilerParams(vmem_limit_bytes=VMEM_LIMIT)


def cost(microseconds, flops=0):
    moved = int(microseconds * 1e3)
    return pl.CostEstimate(flops=flops, bytes_accessed=moved, transcendentals=0)


def floats(rows):
    return jax.ShapeDtypeStruct((rows, LANES), jnp.float32)


def partner(i, k, size):
    return i ^ k if size & (size - 1) == 0 else (k - i) % size


def exchange(parts, size):
    return [parts[0] if size & (size - 1) == 0 else lax.ppermute(parts[0], "plane", pairs_of(0, size))] + [
        lax.ppermute(parts[k], "plane", pairs_of(k, size)) for k in range(1, size)
    ]


def pairs_of(k, size):
    return [(i, partner(i, k, size)) for i in range(size)]


def local(orbitals, kernel_half, pair_own, pair_step, pair_remote, pair_count):
    groups, blocks, planes = (lax.axis_size(name) for name in ("groups", "blk", "plane"))
    orbs, depth, cell_count = orbitals.shape
    slots = pair_own.shape[0]
    lines = cell_count // LANES
    flat = orbitals.reshape(orbs * lines, LANES)
    shares, late = shares_for(slots, planes)

    width = -(-(slots + 1) // LANES) * LANES
    *requests, known = pl.pallas_call(
        functools.partial(plan_kernel, slots, orbs, late),
        out_shape=(
            *[jax.ShapeDtypeStruct((width,), jnp.int32)] * STEPS,
            jax.ShapeDtypeStruct((3 * slots,), jnp.int32),
        ),
        in_specs=[smem] * 4,
        out_specs=(smem,) * (STEPS + 1),
        scratch_shapes=[
            pltpu.SMEM((STEPS * orbs,), jnp.int32),
            pltpu.SMEM((slots + STEPS,), jnp.int32),
        ],
        cost_estimate=cost(2.3),
        name="plan",
    )(pair_own, pair_step, pair_remote, pair_count)

    wanted = [lax.ppermute(requests[s], "blk", route(-s - 1, blocks)) for s in range(STEPS)]

    def send(low, high, flat, wanted):
        packs = [
            pl.pallas_call(
                functools.partial(pack_kernel, lines, low, high),
                out_shape=floats((high - low) * lines),
                in_specs=[smem, vmem],
                out_specs=vmem,
                compiler_params=params(),
                cost_estimate=cost(0.5),
                name="pack",
            )(wanted[s], flat)
            for s in range(STEPS)
        ]
        return packs, [lax.ppermute(packs[s], "blk", route(s + 1, blocks)) for s in range(STEPS)]

    def make_density(bounds, base, size, place, owned, received, after):
        each = size // planes
        return pl.pallas_call(
            functools.partial(density_kernel, slots, lines, planes, bounds, base, size),
            out_shape=[floats(each * lines)] * planes + [floats(size * lines)],
            in_specs=[smem, vmem] + [vmem] * len(received) + [hbm] * len(after),
            out_specs=[vmem] * (planes + 1),
            compiler_params=params(),
            cost_estimate=cost(0.05 * size),
            name="density",
        )(place, owned, *received, *after)

    def filter_parts(parts, kernel, tables):
        each = parts[0].shape[0] // lines
        backs = pl.pallas_call(
            functools.partial(transform_kernel, each, lines, planes),
            out_shape=[floats(each * lines)] * planes,
            in_specs=[vmem] * (planes + 9),
            out_specs=[vmem] * planes,
            scratch_shapes=[
                pltpu.VMEM((each * planes * lines, LANES), jnp.float32),
                pltpu.VMEM((each, NG, NG), jnp.float32),
                pltpu.VMEM((each * planes * lines, LANES), jnp.float32),
            ],
            compiler_params=params(),
            cost_estimate=cost(0.5 + 0.4 * each),
            name="transform",
        )(*exchange(parts, planes), *tables, kernel)
        return backs

    def add_up(base, size, place, kept, potentials, before):
        return pl.pallas_call(
            functools.partial(sum_kernel, slots, lines, planes, base, size, not before),
            out_shape=floats(orbs * lines),
            in_specs=[smem] + [vmem] * (planes + 1 + len(before)),
            out_specs=vmem,
            compiler_params=params(),
            cost_estimate=cost(0.9),
            name="sum",
        )(place, kept, *potentials, *before)

    def own_rows(c, place, flat):
        return pl.pallas_call(
            functools.partial(own_kernel, slots, lines, sum(shares[:c]), shares[c]),
            out_shape=floats(shares[c] * lines),
            in_specs=[smem, vmem],
            out_specs=vmem,
            compiler_params=params(),
            cost_estimate=cost(0.5),
            name="own",
        )(place, flat)

    def one_chunk(bounds, c, place, owned, kernel, tables, received, before, after=()):
        base, size = sum(shares[:c]), shares[c]
        *parts, kept = make_density(bounds, base, size, place, owned[c], received, after)
        backs = filter_parts(parts, kernel, tables)
        potentials = exchange(backs, planes)
        return add_up(base, size, place, kept, potentials, before), potentials

    packs, first = send(0, FIRST, flat, wanted)
    place, choice = pl.pallas_call(
        functools.partial(place_kernel, slots, planes, shares),
        out_shape=(
            jax.ShapeDtypeStruct((3 * slots,), jnp.int32),
            jax.ShapeDtypeStruct((1,), jnp.int32),
        ),
        in_specs=[smem] * (STEPS + 2) + [hbm] * STEPS,
        out_specs=(smem, smem),
        scratch_shapes=[pltpu.SMEM((slots,), jnp.int32), pltpu.SMEM((2,), jnp.int32)],
        cost_estimate=cost(2.8),
        name="place",
    )(known, requests[0], *wanted, *packs)
    packed = pl.pallas_call(
        functools.partial(packs_kernel, lines),
        out_shape=[floats((t - FIRST) * lines) for t in TOTALS for s in range(STEPS)],
        in_specs=[smem] * STEPS + [vmem],
        out_specs=[vmem] * (STEPS * len(TOTALS)),
        compiler_params=params(),
        cost_estimate=cost(2),
        name="packs",
    )(*wanted, flat)
    owned = [own_rows(c, place, flat) for c in range(len(shares))]
    kernel = pl.pallas_call(
        expand_kernel,
        out_shape=jax.ShapeDtypeStruct((NG, NG), jnp.float32),
        in_specs=[vmem],
        out_specs=vmem,
        cost_estimate=cost(1.4),
        name="expand",
    )(kernel_half)
    if is_ring(blocks) and groups == 2:
        choice = jnp.maximum(choice, lax.ppermute(choice, "groups", [(0, 1), (1, 0)]))
    else:
        choice = lax.pmax(choice, ("groups", "blk"))
    tables = [jnp.asarray(part) for pair in make_tables(NG // planes) for part in pair]

    def finish(total, flat, wanted, packed, place, owned, kernel, tables, first):
        i = TOTALS.index(total)
        packs = packed[i * STEPS : (i + 1) * STEPS]
        later = [lax.ppermute(packs[s], "blk", route(s + 1, blocks)) for s in range(STEPS)]
        summed, after, formed = [], [], []
        for c in range(len(shares)):
            early = c < len(EARLY)
            bounds = (FIRST,) if early else (FIRST, total)
            rows = first if early else first + later
            result, potentials = one_chunk(
                bounds, c, place, owned, kernel, tables, rows, summed, after
            )
            summed = [result]
            if early:
                formed += potentials[1 if total - FIRST > 9 else 2 :]
            if c + 1 == len(EARLY):
                after = formed
        return summed[0]

    def general(flat, wanted, packed, place, owned, kernel, tables, first):
        rows = send(0, slots, flat, wanted)[1]
        summed = []
        for c in range(len(shares)):
            summed = [one_chunk((slots,), c, place, owned, kernel, tables, rows, summed)[0]]
        return summed[0]

    summed = lax.switch(
        choice[0],
        [functools.partial(finish, total) for total in TOTALS] + [general],
        flat,
        wanted,
        packed,
        place,
        owned,
        kernel,
        tables,
        first,
    )
    return summed.reshape(orbs, depth, cell_count)


def solution(mesh):
    in_specs = (
        P(("groups", "blk"), None, "plane"),
        P(),
        P(("groups", "blk")),
        P(("groups", "blk")),
        P(("groups", "blk")),
        P(("groups", "blk")),
    )
    out_specs = P(("groups", "blk"), None, "plane")
    return jax.shard_map(local, mesh=mesh, in_specs=in_specs, out_specs=out_specs, check_vma=False)
```

profile of v0, /device:TPU:9, one launch (start us, length us, event | category | flops | bytes accessed | tf_op | source)
XLA Modules:
  0.0 80.5 jit_solution(16543293638209786588)
XLA Ops:
  0.8 2.3 %plan.1 = (s32[128]{0:T(128)}, s32[128]{0:T(128)}, s32[128]{0:T(128)}, s32[144]{0:T(256)}) custom-call(s32[48]{0:T(128)} %own.4, s32[48]{0:T(128)} %step.1, s32[48]{0:T(128)} %remote.1, s32[1]{0:T(128)S(6)} %copy.32.count), custom_call_target="tpu_custom_call" | custom-call | bytes 2300 | tf_op jit(solution)/shard_map/plan/pallas_call | solution.py:327
  3.2 2.5 %collective-permute-start.106 = (s32[128]{0:T(128)}, s32[128]{0:T(128)S(1)}, u32[]{:S(2)}, u32[]{:S(2)}) collective-permute-start(s32[128]{0:T(128)} %get-tuple-element.446), channel_id=1, source_target_pairs={{0,8},{4,12},{8,0},{12,4},{1,9},{5,13},{9,1},{13,5},{2,10},{6,14},... | collective-permute-start | bytes 1544 | tf_op jit(solution)/shard_map/ppermute | solution.py:343
  5.7 2.2 %collective-permute-start.107 = (s32[128]{0:T(128)}, s32[128]{0:T(128)S(1)}, u32[]{:S(2)}, u32[]{:S(2)}) collective-permute-start(s32[128]{0:T(128)} %get-tuple-element.447), channel_id=1, source_target_pairs={{0,4},{4,8},{8,12},{12,0},{1,5},{5,9},{9,13},{13,1},{2,6},{6,10},{... | collective-permute-start | bytes 1544 | tf_op jit(solution)/shard_map/ppermute | solution.py:343
  7.9 1.5 %pack.9.refs_4_ = f32[400,128]{1,0:T(8,128)S(1)} custom-call(s32[128]{0:T(128)S(1)} %collective-permute-done.105.wanted.refs_1_.refs_0_, f32[3200,128]{1,0:T(8,128)} %bitcast.7), custom_call_target="tpu_custom_call" | custom-call | bytes 500 | tf_op jit(solution)/shard_map/pack/pallas_call | solution.py:347
  10.0 2.1 %collective-permute-start.110 = (f32[400,128]{1,0:T(8,128)S(1)}, f32[400,128]{1,0:T(8,128)}, u32[]{:S(2)}, u32[]{:S(2)}) collective-permute-start(f32[400,128]{1,0:T(8,128)S(1)} %pack.10.refs_5_), channel_id=1, source_target_pairs={{0,8},{4,12},{8,0},{12,4},{1,9},{5,13},{9,1},{13,5},{2,10},{6,14},... | collective-permute-start | bytes 614408 | tf_op jit(solution)/shard_map/ppermute | solution.py:358
  12.7 1.5 %collective-permute-start.111 = (f32[400,128]{1,0:T(8,128)S(1)}, f32[400,128]{1,0:T(8,128)}, u32[]{:S(2)}, u32[]{:S(2)}) collective-permute-start(f32[400,128]{1,0:T(8,128)S(1)} %pack.11.refs_6_), channel_id=1, source_target_pairs={{0,12},{4,0},{8,4},{12,8},{1,13},{5,1},{9,5},{13,9},{2,14},{6,2},{... | collective-permute-start | bytes 614408 | tf_op jit(solution)/shard_map/ppermute | solution.py:358
  14.8 1.3 %expand.1 = f32[160,160]{1,0:T(8,128)S(1)} custom-call(f32[1,81,81]{2,1,0:T(8,128)} %copy.20.half), custom_call_target="tpu_custom_call" | custom-call | bytes 1400 | tf_op jit(solution)/shard_map/expand/pallas_call | solution.py:442
  16.2 2.6 %place.1 = (s32[144]{0:T(256)S(1)}, s32[1]{0:T(128)}) custom-call(s32[144]{0:T(256)} %get-tuple-element.444.known, s32[128]{0:T(128)} %get-tuple-element.445.refs_0_, s32[128]{0:T(128)S(1)} %collective-permute-done.105.wanted.refs_1_.refs_0_, s32[128]{0:T(128)S(1)} %collective-permute-done.106.wanted.refs_2_.refs_1_, ...), custom_call_target="tpu_custom_call" | custom-call | bytes 2800 | tf_op jit(solution)/shard_map/place/pallas_call | solution.py:420
  25.8 4.5 %collective-permute-done.111 = f32[400,128]{1,0:T(8,128)} collective-permute-done((f32[400,128]{1,0:T(8,128)S(1)}, f32[400,128]{1,0:T(8,128)}, u32[]{:S(2)}, u32[]{:S(2)}) %collective-permute-start.111) | collective-permute-done | bytes 204832 | tf_op jit(solution)/shard_map/ppermute | solution.py:358
  30.4 49.0 %conditional.1 = (f32[64,1,6400]{2,1,0:T(1,128)S(1)}) conditional(s32[]{:T(128)} %bitcast.6, (f32[450,128]{1,0:T(8,128)S(1)}, f32[450,128]{1,0:T(8,128)S(1)}, f32[450,128]{1,0:T(8,128)S(1)}, s32[144]{0:T(256)S(1)}, f32[1200,128]{1,0:T(8,128)S(1)}, /*index=5*/f32[400,128]{1,0:T(8,128)}, f32[400,128]{1,0:T(8,128)}, ...), branch_computations={%region_0.0_spmd, %region_1.0_spmd, %region_2.0_spmd, %region_3.0_... | conditional | bytes 22132148 | solution.py:482
  30.4 1.3 %density.15 = (f32[300,128]{1,0:T(8,128)S(1)}, f32[300,128]{1,0:T(8,128)S(1)}, f32[300,128]{1,0:T(8,128)S(1)}, f32[300,128]{1,0:T(8,128)S(1)}, f32[1200,128]{1,0:T(8,128)S(1)}) custom-call(s32[144]{0:T(256)S(1)} %get-tuple-element.196.place, f32[1200,128]{1,0:T(8,128)S(1)} %get-tuple-element.206.owned, f32[400,128]{1,0:T(8,128)} %get-tuple-element.200.refs_0_, ...), custom_call_target="tpu_custom_call" | custom-call | bytes 1200 | tf_op jit(solution)/shard_map/cond/branch_0_fun/density/pallas_call | solution.py:362
  34.3 1.5 %collective-permute-start.2 = (f32[450,128]{1,0:T(8,128)S(1)}, f32[450,128]{1,0:T(8,128)S(1)}, u32[]{:S(2)}, u32[]{:S(2)}) collective-permute-start(f32[450,128]{1,0:T(8,128)S(1)} %get-tuple-element.205), channel_id=1, source_target_pairs={{0,12},{4,0},{8,4},{12,8},{1,13},{5,1},{9,5},{13,9},{2,14},{6,2},{... | collective-permute-start | bytes 691208 | tf_op jit(solution)/shard_map/cond/branch_0_fun/ppermute | solution.py:459
  35.8 2.1 %collective-permute-done.4.refs_2_ = f32[300,128]{1,0:T(8,128)S(1)} collective-permute-done((f32[300,128]{1,0:T(8,128)S(1)}, f32[300,128]{1,0:T(8,128)S(1)}, u32[]{:S(2)}, u32[]{:S(2)}) %collective-permute-start.4) | collective-permute-done | bytes 153632 | tf_op jit(solution)/shard_map/cond/branch_0_fun/ppermute | solution.py:310
  37.9 3.8 %collective-permute-done.5.refs_3_ = f32[300,128]{1,0:T(8,128)S(1)} collective-permute-done((f32[300,128]{1,0:T(8,128)S(1)}, f32[300,128]{1,0:T(8,128)S(1)}, u32[]{:S(2)}, u32[]{:S(2)}) %collective-permute-start.5) | collective-permute-done | bytes 153632 | tf_op jit(solution)/shard_map/cond/branch_0_fun/ppermute | solution.py:310
  41.7 2.7 %transform.15 = (f32[300,128]{1,0:T(8,128)S(1)}, f32[300,128]{1,0:T(8,128)S(1)}, f32[300,128]{1,0:T(8,128)S(1)}, f32[300,128]{1,0:T(8,128)S(1)}) custom-call(f32[300,128]{1,0:T(8,128)S(1)} %get-tuple-element.207.refs_0_, f32[300,128]{1,0:T(8,128)S(1)} %collective-permute-done.3.refs_1_, f32[300,128]{1,0:T(8,128)S(1)} %collective-permute-done.4.refs_2_, ...), custom_call_target="tpu_custom_call" | custom-call | bytes 2900 | tf_op jit(solution)/shard_map/cond/branch_0_fun/transform/pallas_call | solution.py:374
  46.0 8.2 %collective-permute-done.1.refs_4_ = f32[450,128]{1,0:T(8,128)S(1)} collective-permute-done((f32[450,128]{1,0:T(8,128)S(1)}, f32[450,128]{1,0:T(8,128)S(1)}, u32[]{:S(2)}, u32[]{:S(2)}) %collective-permute-start.1) | collective-permute-done | bytes 230432 | tf_op jit(solution)/shard_map/cond/branch_0_fun/ppermute | solution.py:459
  54.1 1.3 %collective-permute-done.2.refs_5_ = f32[450,128]{1,0:T(8,128)S(1)} collective-permute-done((f32[450,128]{1,0:T(8,128)S(1)}, f32[450,128]{1,0:T(8,128)S(1)}, u32[]{:S(2)}, u32[]{:S(2)}) %collective-permute-start.2) | collective-permute-done | bytes 230432 | tf_op jit(solution)/shard_map/cond/branch_0_fun/ppermute | solution.py:459
  55.5 1.3 %density.17 = (f32[150,128]{1,0:T(8,128)S(1)}, f32[150,128]{1,0:T(8,128)S(1)}, f32[150,128]{1,0:T(8,128)S(1)}, f32[150,128]{1,0:T(8,128)S(1)}, f32[600,128]{1,0:T(8,128)S(1)}) custom-call(s32[144]{0:T(256)S(1)} %get-tuple-element.196.place, f32[600,128]{1,0:T(8,128)S(1)} %get-tuple-element.231.owned, f32[400,128]{1,0:T(8,128)} %get-tuple-element.200.refs_0_, ...), custom_call_target="tpu_custom_call" | custom-call | bytes 600 | tf_op jit(solution)/shard_map/cond/branch_0_fun/density/pallas_call | solution.py:362
  62.2 1.5 %collective-permute-start.10 = (f32[150,128]{1,0:T(8,128)S(1)}, f32[150,128]{1,0:T(8,128)S(1)}, u32[]{:S(2)}, u32[]{:S(2)}) collective-permute-start(f32[150,128]{1,0:T(8,128)S(1)} %get-tuple-element.226), channel_id=1, source_target_pairs={{0,3},{1,2},{2,1},{3,0},{4,7},{5,6},{6,5},{7,4},{8,11},{9,10},{10,... | collective-permute-start | bytes 230408 | tf_op jit(solution)/shard_map/cond/branch_0_fun/ppermute | solution.py:310
  63.7 1.5 %transform.17 = (f32[150,128]{1,0:T(8,128)S(1)}, f32[150,128]{1,0:T(8,128)S(1)}, f32[150,128]{1,0:T(8,128)S(1)}, f32[150,128]{1,0:T(8,128)S(1)}) custom-call(f32[150,128]{1,0:T(8,128)S(1)} %get-tuple-element.233.refs_0_, f32[150,128]{1,0:T(8,128)S(1)} %collective-permute-done.14.refs_1_, f32[150,128]{1,0:T(8,128)S(1)} %collective-permute-done.15.refs_2_, ...), custom_call_target="tpu_custom_call" | custom-call | bytes 1700 | tf_op jit(solution)/shard_map/cond/branch_0_fun/transform/pallas_call | solution.py:374
  65.3 1.6 %collective-permute-done.10.refs_3_ = f32[150,128]{1,0:T(8,128)S(1)} collective-permute-done((f32[150,128]{1,0:T(8,128)S(1)}, f32[150,128]{1,0:T(8,128)S(1)}, u32[]{:S(2)}, u32[]{:S(2)}) %collective-permute-start.10) | collective-permute-done | bytes 76832 | tf_op jit(solution)/shard_map/cond/branch_0_fun/ppermute | solution.py:310
  66.9 1.5 %transform.16 = (f32[150,128]{1,0:T(8,128)S(1)}, f32[150,128]{1,0:T(8,128)S(1)}, f32[150,128]{1,0:T(8,128)S(1)}, f32[150,128]{1,0:T(8,128)S(1)}) custom-call(f32[150,128]{1,0:T(8,128)S(1)} %get-tuple-element.223.refs_0_, f32[150,128]{1,0:T(8,128)S(1)} %collective-permute-done.8.refs_1_, f32[150,128]{1,0:T(8,128)S(1)} %collective-permute-done.9.refs_2_, ...), custom_call_target="tpu_custom_call" | custom-call | bytes 1700 | tf_op jit(solution)/shard_map/cond/branch_0_fun/transform/pallas_call | solution.py:374
  73.3 1.5 %collective-permute-done.19.refs_4_ = f32[150,128]{1,0:T(8,128)S(1)} collective-permute-done((f32[150,128]{1,0:T(8,128)S(1)}, f32[150,128]{1,0:T(8,128)S(1)}, u32[]{:S(2)}, u32[]{:S(2)}) %collective-permute-start.19) | collective-permute-done | bytes 76832 | tf_op jit(solution)/shard_map/cond/branch_0_fun/ppermute | solution.py:310
  76.3 1.7 %collective-permute-done.13.refs_4_ = f32[150,128]{1,0:T(8,128)S(1)} collective-permute-done((f32[150,128]{1,0:T(8,128)S(1)}, f32[150,128]{1,0:T(8,128)S(1)}, u32[]{:S(2)}, u32[]{:S(2)}) %collective-permute-start.13) | collective-permute-done | bytes 76832 | tf_op jit(solution)/shard_map/cond/branch_0_fun/ppermute | solution.py:310
  (89 shorter events, 25.5 us)
Async XLA Ops:
  3.1 4.7 %collective-permute-start.105 = (s32[128]{0:T(128)}, s32[128]{0:T(128)S(1)}, u32[]{:S(2)}, u32[]{:S(2)}) collective-permute-start(s32[128]{0:T(128)} %get-tuple-element.445.refs_0_), channel_id=1, source_target_pairs={{0,12},{4,0},{8,4},{12,8},{1,13},{5,1},{9,5},{13,9},{2,14},{6,2},{... | collective-permute-start | bytes 1544 | tf_op jit(solution)/shard_map/ppermute | solution.py:343
  3.2 6.2 %collective-permute-start.106 = (s32[128]{0:T(128)}, s32[128]{0:T(128)S(1)}, u32[]{:S(2)}, u32[]{:S(2)}) collective-permute-start(s32[128]{0:T(128)} %get-tuple-element.446), channel_id=1, source_target_pairs={{0,8},{4,12},{8,0},{12,4},{1,9},{5,13},{9,1},{13,5},{2,10},{6,14},... | collective-permute-start | bytes 1544 | tf_op jit(solution)/shard_map/ppermute | solution.py:343
  5.7 6.5 %collective-permute-start.107 = (s32[128]{0:T(128)}, s32[128]{0:T(128)S(1)}, u32[]{:S(2)}, u32[]{:S(2)}) collective-permute-start(s32[128]{0:T(128)} %get-tuple-element.447), channel_id=1, source_target_pairs={{0,4},{4,8},{8,12},{12,0},{1,5},{5,9},{9,13},{13,1},{2,6},{6,10},{... | collective-permute-start | bytes 1544 | tf_op jit(solution)/shard_map/ppermute | solution.py:343
  9.4 15.5 %collective-permute-start.109 = (f32[400,128]{1,0:T(8,128)S(1)}, f32[400,128]{1,0:T(8,128)}, u32[]{:S(2)}, u32[]{:S(2)}) collective-permute-start(f32[400,128]{1,0:T(8,128)S(1)} %pack.9.refs_4_), channel_id=1, source_target_pairs={{0,4},{4,8},{8,12},{12,0},{1,5},{5,9},{9,13},{13,1},{2,6},{6,10},{... | collective-permute-start | bytes 614408 | tf_op jit(solution)/shard_map/ppermute | solution.py:358
  10.0 15.8 %collective-permute-start.110 = (f32[400,128]{1,0:T(8,128)S(1)}, f32[400,128]{1,0:T(8,128)}, u32[]{:S(2)}, u32[]{:S(2)}) collective-permute-start(f32[400,128]{1,0:T(8,128)S(1)} %pack.10.refs_5_), channel_id=1, source_target_pairs={{0,8},{4,12},{8,0},{12,4},{1,9},{5,13},{9,1},{13,5},{2,10},{6,14},... | collective-permute-start | bytes 614408 | tf_op jit(solution)/shard_map/ppermute | solution.py:358
  12.7 17.6 %collective-permute-start.111 = (f32[400,128]{1,0:T(8,128)S(1)}, f32[400,128]{1,0:T(8,128)}, u32[]{:S(2)}, u32[]{:S(2)}) collective-permute-start(f32[400,128]{1,0:T(8,128)S(1)} %pack.11.refs_6_), channel_id=1, source_target_pairs={{0,12},{4,0},{8,4},{12,8},{1,13},{5,1},{9,5},{13,9},{2,14},{6,2},{... | collective-permute-start | bytes 614408 | tf_op jit(solution)/shard_map/ppermute | solution.py:358
  32.3 5.6 %collective-permute-start.4 = (f32[300,128]{1,0:T(8,128)S(1)}, f32[300,128]{1,0:T(8,128)S(1)}, u32[]{:S(2)}, u32[]{:S(2)}) collective-permute-start(f32[300,128]{1,0:T(8,128)S(1)} %get-tuple-element.209), channel_id=1, source_target_pairs={{0,2},{1,3},{2,0},{3,1},{4,6},{5,7},{6,4},{7,5},{8,10},{9,11},{10,... | collective-permute-start | bytes 460808 | tf_op jit(solution)/shard_map/cond/branch_0_fun/ppermute | solution.py:310
  33.5 8.2 %collective-permute-start.5 = (f32[300,128]{1,0:T(8,128)S(1)}, f32[300,128]{1,0:T(8,128)S(1)}, u32[]{:S(2)}, u32[]{:S(2)}) collective-permute-start(f32[300,128]{1,0:T(8,128)S(1)} %get-tuple-element.210), channel_id=1, source_target_pairs={{0,3},{1,2},{2,1},{3,0},{4,7},{5,6},{6,5},{7,4},{8,11},{9,10},{10,... | collective-permute-start | bytes 460808 | tf_op jit(solution)/shard_map/cond/branch_0_fun/ppermute | solution.py:310
  34.0 12.0 %collective-permute-start = (f32[450,128]{1,0:T(8,128)S(1)}, f32[450,128]{1,0:T(8,128)S(1)}, u32[]{:S(2)}, u32[]{:S(2)}) collective-permute-start(f32[450,128]{1,0:T(8,128)S(1)} %get-tuple-element.203), channel_id=1, source_target_pairs={{0,4},{4,8},{8,12},{12,0},{1,5},{5,9},{9,13},{13,1},{2,6},{6,10},{... | collective-permute-start | bytes 691208 | tf_op jit(solution)/shard_map/cond/branch_0_fun/ppermute | solution.py:459
  34.0 20.2 %collective-permute-start.1 = (f32[450,128]{1,0:T(8,128)S(1)}, f32[450,128]{1,0:T(8,128)S(1)}, u32[]{:S(2)}, u32[]{:S(2)}) collective-permute-start(f32[450,128]{1,0:T(8,128)S(1)} %get-tuple-element.204), channel_id=1, source_target_pairs={{0,8},{4,12},{8,0},{12,4},{1,9},{5,13},{9,1},{13,5},{2,10},{6,14},... | collective-permute-start | bytes 691208 | tf_op jit(solution)/shard_map/cond/branch_0_fun/ppermute | solution.py:459
  34.3 21.2 %collective-permute-start.2 = (f32[450,128]{1,0:T(8,128)S(1)}, f32[450,128]{1,0:T(8,128)S(1)}, u32[]{:S(2)}, u32[]{:S(2)}) collective-permute-start(f32[450,128]{1,0:T(8,128)S(1)} %get-tuple-element.205), channel_id=1, source_target_pairs={{0,12},{4,0},{8,4},{12,8},{1,13},{5,1},{9,5},{13,9},{2,14},{6,2},{... | collective-permute-start | bytes 691208 | tf_op jit(solution)/shard_map/cond/branch_0_fun/ppermute | solution.py:459
  44.4 11.1 %collective-permute-start.6 = (f32[300,128]{1,0:T(8,128)S(1)}, f32[300,128]{1,0:T(8,128)S(1)}, u32[]{:S(2)}, u32[]{:S(2)}) collective-permute-start(f32[300,128]{1,0:T(8,128)S(1)} %get-tuple-element.220), channel_id=1, source_target_pairs={{0,2},{1,3},{2,0},{3,1},{4,6},{5,7},{6,4},{7,5},{8,10},{9,11},{10,... | collective-permute-start | bytes 460808 | tf_op jit(solution)/shard_map/cond/branch_0_fun/ppermute | solution.py:310
  45.6 9.9 %collective-permute-start.7 = (f32[300,128]{1,0:T(8,128)S(1)}, f32[300,128]{1,0:T(8,128)S(1)}, u32[]{:S(2)}, u32[]{:S(2)}) collective-permute-start(f32[300,128]{1,0:T(8,128)S(1)} %get-tuple-element.221), channel_id=1, source_target_pairs={{0,3},{1,2},{2,1},{3,0},{4,7},{5,6},{6,5},{7,4},{8,11},{9,10},{10,... | collective-permute-start | bytes 460808 | tf_op jit(solution)/shard_map/cond/branch_0_fun/ppermute | solution.py:310
  57.4 4.8 %collective-permute-start.15 = (f32[150,128]{1,0:T(8,128)S(1)}, f32[150,128]{1,0:T(8,128)S(1)}, u32[]{:S(2)}, u32[]{:S(2)}) collective-permute-start(f32[150,128]{1,0:T(8,128)S(1)} %get-tuple-element.235), channel_id=1, source_target_pairs={{0,2},{1,3},{2,0},{3,1},{4,6},{5,7},{6,4},{7,5},{8,10},{9,11},{10,... | collective-permute-start | bytes 230408 | tf_op jit(solution)/shard_map/cond/branch_0_fun/ppermute | solution.py:310
  58.6 5.1 %collective-permute-start.16 = (f32[150,128]{1,0:T(8,128)S(1)}, f32[150,128]{1,0:T(8,128)S(1)}, u32[]{:S(2)}, u32[]{:S(2)}) collective-permute-start(f32[150,128]{1,0:T(8,128)S(1)} %get-tuple-element.236), channel_id=1, source_target_pairs={{0,3},{1,2},{2,1},{3,0},{4,7},{5,6},{6,5},{7,4},{8,11},{9,10},{10,... | collective-permute-start | bytes 230408 | tf_op jit(solution)/shard_map/cond/branch_0_fun/ppermute | solution.py:310
  59.1 11.5 %collective-permute-start.20 = (f32[300,128]{1,0:T(8,128)S(1)}, f32[300,128]{1,0:T(8,128)S(1)}, u32[]{:S(2)}, u32[]{:S(2)}) collective-permute-start(f32[300,128]{1,0:T(8,128)S(1)} %get-tuple-element.243), channel_id=1, source_target_pairs={{0,1},{1,0},{2,3},{3,2},{4,5},{5,4},{6,7},{7,6},{8,9},{9,8},{10,11... | collective-permute-start | bytes 460808 | tf_op jit(solution)/shard_map/cond/branch_0_fun/ppermute | solution.py:310
  60.6 4.7 %collective-permute-start.8 = (f32[150,128]{1,0:T(8,128)S(1)}, f32[150,128]{1,0:T(8,128)S(1)}, u32[]{:S(2)}, u32[]{:S(2)}) collective-permute-start(f32[150,128]{1,0:T(8,128)S(1)} %get-tuple-element.224), channel_id=1, source_target_pairs={{0,1},{1,0},{2,3},{3,2},{4,5},{5,4},{6,7},{7,6},{8,9},{9,8},{10,11... | collective-permute-start | bytes 230408 | tf_op jit(solution)/shard_map/cond/branch_0_fun/ppermute | solution.py:310
  62.2 4.7 %collective-permute-start.10 = (f32[150,128]{1,0:T(8,128)S(1)}, f32[150,128]{1,0:T(8,128)S(1)}, u32[]{:S(2)}, u32[]{:S(2)}) collective-permute-start(f32[150,128]{1,0:T(8,128)S(1)} %get-tuple-element.226), channel_id=1, source_target_pairs={{0,3},{1,2},{2,1},{3,0},{4,7},{5,6},{6,5},{7,4},{8,11},{9,10},{10,... | collective-permute-start | bytes 230408 | tf_op jit(solution)/shard_map/cond/branch_0_fun/ppermute | solution.py:310
  65.2 6.6 %collective-permute-start.17 = (f32[150,128]{1,0:T(8,128)S(1)}, f32[150,128]{1,0:T(8,128)S(1)}, u32[]{:S(2)}, u32[]{:S(2)}) collective-permute-start(f32[150,128]{1,0:T(8,128)S(1)} %get-tuple-element.238), channel_id=1, source_target_pairs={{0,1},{1,0},{2,3},{3,2},{4,5},{5,4},{6,7},{7,6},{8,9},{9,8},{10,11... | collective-permute-start | bytes 230408 | tf_op jit(solution)/shard_map/cond/branch_0_fun/ppermute | solution.py:310
  68.4 7.3 %collective-permute-start.11 = (f32[150,128]{1,0:T(8,128)S(1)}, f32[150,128]{1,0:T(8,128)S(1)}, u32[]{:S(2)}, u32[]{:S(2)}) collective-permute-start(f32[150,128]{1,0:T(8,128)S(1)} %get-tuple-element.228), channel_id=1, source_target_pairs={{0,1},{1,0},{2,3},{3,2},{4,5},{5,4},{6,7},{7,6},{8,9},{9,8},{10,11... | collective-permute-start | bytes 230408 | tf_op jit(solution)/shard_map/cond/branch_0_fun/ppermute | solution.py:310
  68.8 4.5 %collective-permute-start.18 = (f32[150,128]{1,0:T(8,128)S(1)}, f32[150,128]{1,0:T(8,128)S(1)}, u32[]{:S(2)}, u32[]{:S(2)}) collective-permute-start(f32[150,128]{1,0:T(8,128)S(1)} %get-tuple-element.239), channel_id=1, source_target_pairs={{0,2},{1,3},{2,0},{3,1},{4,6},{5,7},{6,4},{7,5},{8,10},{9,11},{10,... | collective-permute-start | bytes 230408 | tf_op jit(solution)/shard_map/cond/branch_0_fun/ppermute | solution.py:310
  70.0 4.8 %collective-permute-start.19 = (f32[150,128]{1,0:T(8,128)S(1)}, f32[150,128]{1,0:T(8,128)S(1)}, u32[]{:S(2)}, u32[]{:S(2)}) collective-permute-start(f32[150,128]{1,0:T(8,128)S(1)} %get-tuple-element.240), channel_id=1, source_target_pairs={{0,3},{1,2},{2,1},{3,0},{4,7},{5,6},{6,5},{7,4},{8,11},{9,10},{10,... | collective-permute-start | bytes 230408 | tf_op jit(solution)/shard_map/cond/branch_0_fun/ppermute | solution.py:310
  70.6 5.8 %collective-permute-start.12 = (f32[150,128]{1,0:T(8,128)S(1)}, f32[150,128]{1,0:T(8,128)S(1)}, u32[]{:S(2)}, u32[]{:S(2)}) collective-permute-start(f32[150,128]{1,0:T(8,128)S(1)} %get-tuple-element.229), channel_id=1, source_target_pairs={{0,2},{1,3},{2,0},{3,1},{4,6},{5,7},{6,4},{7,5},{8,10},{9,11},{10,... | collective-permute-start | bytes 230408 | tf_op jit(solution)/shard_map/cond/branch_0_fun/ppermute | solution.py:310
  71.8 6.2 %collective-permute-start.13 = (f32[150,128]{1,0:T(8,128)S(1)}, f32[150,128]{1,0:T(8,128)S(1)}, u32[]{:S(2)}, u32[]{:S(2)}) collective-permute-start(f32[150,128]{1,0:T(8,128)S(1)} %get-tuple-element.230), channel_id=1, source_target_pairs={{0,3},{1,2},{2,1},{3,0},{4,7},{5,6},{6,5},{7,4},{8,11},{9,10},{10,... | collective-permute-start | bytes 230408 | tf_op jit(solution)/shard_map/cond/branch_0_fun/ppermute | solution.py:310
  (22 other events, 151.4 us)
where the time goes:
time: 80.4 us; the launch traced here: 80.5 us
  waiting for transfers between devices  26.9 us (33%)
  starting transfers between devices  25 us (31%)
  Pallas kernels  23.7 us (29%)
  between operations  2.49 us (3%)
  local copies, waits for them, and re-layouts  1.87 us (2%)
    ppermute x18, starting transfers between devices, exchange(): lax.ppermute(parts[k], 'plane', pairs_of(k, size))  13.5 us
    ppermute x18, waiting for transfers between devices, exchange(): lax.ppermute(parts[k], 'plane', pairs_of(k, size))  11.4 us
    ppermute x3, waiting for transfers between devices, finish(): lax.ppermute(packs[s], 'blk', route(s + 1, blocks))  9.5 us
    pallas_call x3, Pallas kernels, filter_parts(): pl.pallas_call(functools.partial(transform_kernel, each, lines, planes),...  5.64 us
    ppermute x3, waiting for transfers between devices, send(): lax.ppermute(packs[s], 'blk', route(s + 1, blocks))  5.38 us
    ppermute x3, starting transfers between devices, local(): lax.ppermute(requests[s], 'blk', route(-s - 1, blocks))  4.72 us
    pallas_call x3, Pallas kernels, make_density(): pl.pallas_call(functools.partial(density_kernel, slots, lines, planes, bo...  3.97 us
    ppermute x3, starting transfers between devices, send(): lax.ppermute(packs[s], 'blk', route(s + 1, blocks))  3.64 us
  transfers between devices with their start and end apart: 28, of which 11 were waited for; matrix products, arithmetic and copies ran while one was open for 1% of the time, Pallas kernels for 22%

commit v1 on v0

--- a/solution.py
+++ b/solution.py
@@ -174,26 +174,37 @@
         base += size
 
 
+def pieces(lines):
+    whole = lines // 8 * 8
+    return [(0, whole)] + ([(lines - 8, 8)] if whole < lines else [])
+
+
+def move_row(source, at, target, to, lines):
+    for start, size in pieces(lines):
+        target[pl.ds(to + start, size), :] = source[pl.ds(at + start, size), :]
+
+
 def pack_kernel(lines, low, high, wanted, orbitals, sent):
     for c in range(low, high):
-        row = wanted[c] * lines
-        sent[pl.ds((c - low) * lines, lines), :] = orbitals[pl.ds(row, lines), :]
+        move_row(orbitals, wanted[c] * lines, sent, (c - low) * lines, lines)
 
 
 def packs_kernel(lines, *refs):
     wanted, orbitals, sent = refs[:STEPS], refs[STEPS], refs[STEPS + 1 :]
     for s in range(STEPS):
         for c in range(FIRST, TOTALS[-1]):
-            row = orbitals[pl.ds(wanted[s][c] * lines, lines), :]
-            for i, total in enumerate(TOTALS):
-                if c < total:
-                    sent[i * STEPS + s][pl.ds((c - FIRST) * lines, lines), :] = row
+            for start, size in pieces(lines):
+                value = orbitals[pl.ds(wanted[s][c] * lines + start, size), :]
+                to = (c - FIRST) * lines + start
+                for i, total in enumerate(TOTALS):
+                    if c < total:
+                        sent[i * STEPS + s][pl.ds(to, size), :] = value
 
 
 def own_kernel(slots, lines, base, size, place, orbitals, owned):
     for j in range(size):
         near = jnp.maximum(place[2 * slots + base + j], 0) * lines
-        owned[pl.ds(j * lines, lines), :] = orbitals[pl.ds(near, lines), :]
+        move_row(orbitals, near, owned, j * lines, lines)
 
 
 def density_kernel(slots, lines, planes, bounds, base, size, place, owned, *refs):
@@ -201,16 +212,18 @@
     each = size // planes
     for j in range(size):
         s, rank = place[base + j], place[slots + base + j]
-        for c, (low, high) in enumerate(zip((0,) + bounds, bounds)):
-            row = jnp.clip(rank - low, 0, high - low - 1) * lines
-            found = received[c * STEPS][pl.ds(row, lines), :]
-            for i in range(1, STEPS):
-                found = jnp.where(s == i, received[c * STEPS + i][pl.ds(row, lines), :], found)
-            value = found if c == 0 else jnp.where(rank >= low, found, value)
-        kept[pl.ds(j * lines, lines), :] = value
-        parts[j // each][pl.ds(j % each * lines, lines), :] = (
-            owned[pl.ds(j * lines, lines), :] * value
-        )
+        for start, count in pieces(lines):
+            for c, (low, high) in enumerate(zip((0,) + bounds, bounds)):
+                row = jnp.clip(rank - low, 0, high - low - 1) * lines + start
+                found = received[c * STEPS][pl.ds(row, count), :]
+                for i in range(1, STEPS):
+                    other = received[c * STEPS + i][pl.ds(row, count), :]
+                    found = jnp.where(s == i, other, found)
+                value = found if c == 0 else jnp.where(rank >= low, found, value)
+            kept[pl.ds(j * lines + start, count), :] = value
+            parts[j // each][pl.ds(j % each * lines + start, count), :] = (
+                owned[pl.ds(j * lines + start, count), :] * value
+            )
 
 
 def sum_kernel(slots, lines, planes, base, size, fresh, place, *refs):
@@ -226,10 +239,14 @@
 
         @pl.when(near >= 0)
         def _():
-            out[pl.ds(near, lines), :] += (
-                parts[j // each][pl.ds(j % each * lines, lines), :]
-                * kept[pl.ds(j * lines, lines), :]
-            )
+            part, first = parts[j // each], j % each * lines
+            added = [
+                out[pl.ds(near + start, count), :]
+                + part[pl.ds(first + start, count), :] * kept[pl.ds(j * lines + start, count), :]
+                for start, count in pieces(lines)
+            ]
+            for (start, count), value in zip(pieces(lines), added):
+                out[pl.ds(near + start, count), :] = value
 
 
 def transform_kernel(pairs, lines, planes, *refs):
@@ -245,7 +262,7 @@
     for k in range(planes):
         slab = partner(me, k, planes) * lines
         for p in range(pairs):
-            cells[pl.ds(p * whole + slab, lines), :] = parts[k][pl.ds(p * lines, lines), :]
+            move_row(parts[k], p * lines, cells, p * whole + slab, lines)
     line = [split_value(cells[pl.ds(t, pairs * rows, stride=LINES), :]) for t in range(LINES)]
     for r in range(GROUP):
         wide = [jnp.concatenate([line[r][i], line[r + 1][i]], axis=1) for i in range(2)]
@@ -277,7 +294,7 @@
     for k in range(planes):
         slab = partner(me, k, planes) * lines
         for p in range(pairs):
-            outs[k][pl.ds(p * lines, lines), :] = result[pl.ds(p * whole + slab, lines), :]
+            move_row(result, p * whole + slab, outs[k], p * lines, lines)
 
 
 def shares_for(slots, planes):

time: 80.4 us -> 80.9 us (level)
  no operation moved by 1% of the time
where the time goes in v1:
time: 80.9 us; the launch traced here: 80.5 us
  waiting for transfers between devices  26.9 us (33%)
  starting transfers between devices  24.9 us (31%)
  Pallas kernels  23.7 us (29%)
  between operations  2.49 us (3%)
  local copies, waits for them, and re-layouts  1.87 us (2%)
    ppermute x18, starting transfers between devices, exchange(): lax.ppermute(parts[k], 'plane', pairs_of(k, size))  13.5 us
    ppermute x18, waiting for transfers between devices, exchange(): lax.ppermute(parts[k], 'plane', pairs_of(k, size))  11.5 us
    ppermute x3, waiting for transfers between devices, finish(): lax.ppermute(packs[s], 'blk', route(s + 1, blocks))  9.49 us
    pallas_call x3, Pallas kernels, filter_parts(): pl.pallas_call(functools.partial(transform_kernel, each, lines, planes),...  5.65 us
    ppermute x3, waiting for transfers between devices, send(): lax.ppermute(packs[s], 'blk', route(s + 1, blocks))  5.38 us
    ppermute x3, starting transfers between devices, local(): lax.ppermute(requests[s], 'blk', route(-s - 1, blocks))  4.72 us
    pallas_call x3, Pallas kernels, make_density(): pl.pallas_call(functools.partial(density_kernel, slots, lines, planes, bo...  4.06 us
    ppermute x3, starting transfers between devices, send(): lax.ppermute(packs[s], 'blk', route(s + 1, blocks))  3.64 us
  transfers between devices with their start and end apart: 28, of which 11 were waited for; matrix products, arithmetic and copies ran while one was open for 1% of the time, Pallas kernels for 22%

profile of v1, /device:TPU:9, one launch (start us, length us, event | category | flops | bytes accessed | tf_op | source)
XLA Modules:
  0.0 80.5 jit_solution(3969668827854257190)
XLA Ops:
  0.8 2.3 %plan.1 = (s32[128]{0:T(128)}, s32[128]{0:T(128)}, s32[128]{0:T(128)}, s32[144]{0:T(256)}) custom-call(s32[48]{0:T(128)} %own.4, s32[48]{0:T(128)} %step.1, s32[48]{0:T(128)} %remote.1, s32[1]{0:T(128)S(6)} %copy.32.count), custom_call_target="tpu_custom_call" | custom-call | bytes 2300 | tf_op jit(solution)/shard_map/plan/pallas_call | solution.py:344
  3.2 2.5 %collective-permute-start.106 = (s32[128]{0:T(128)}, s32[128]{0:T(128)S(1)}, u32[]{:S(2)}, u32[]{:S(2)}) collective-permute-start(s32[128]{0:T(128)} %get-tuple-element.446), channel_id=1, source_target_pairs={{0,8},{4,12},{8,0},{12,4},{1,9},{5,13},{9,1},{13,5},{2,10},{6,14},... | collective-permute-start | bytes 1544 | tf_op jit(solution)/shard_map/ppermute | solution.py:360
  5.7 2.2 %collective-permute-start.107 = (s32[128]{0:T(128)}, s32[128]{0:T(128)S(1)}, u32[]{:S(2)}, u32[]{:S(2)}) collective-permute-start(s32[128]{0:T(128)} %get-tuple-element.447), channel_id=1, source_target_pairs={{0,4},{4,8},{8,12},{12,0},{1,5},{5,9},{9,13},{13,1},{2,6},{6,10},{... | collective-permute-start | bytes 1544 | tf_op jit(solution)/shard_map/ppermute | solution.py:360
  7.9 1.5 %pack.9.refs_4_ = f32[400,128]{1,0:T(8,128)S(1)} custom-call(s32[128]{0:T(128)S(1)} %collective-permute-done.105.wanted.refs_1_.refs_0_, f32[3200,128]{1,0:T(8,128)} %bitcast.7), custom_call_target="tpu_custom_call" | custom-call | bytes 500 | tf_op jit(solution)/shard_map/pack/pallas_call | solution.py:364
  10.0 2.1 %collective-permute-start.110 = (f32[400,128]{1,0:T(8,128)S(1)}, f32[400,128]{1,0:T(8,128)}, u32[]{:S(2)}, u32[]{:S(2)}) collective-permute-start(f32[400,128]{1,0:T(8,128)S(1)} %pack.10.refs_5_), channel_id=1, source_target_pairs={{0,8},{4,12},{8,0},{12,4},{1,9},{5,13},{9,1},{13,5},{2,10},{6,14},... | collective-permute-start | bytes 614408 | tf_op jit(solution)/shard_map/ppermute | solution.py:375
  12.7 1.5 %collective-permute-start.111 = (f32[400,128]{1,0:T(8,128)S(1)}, f32[400,128]{1,0:T(8,128)}, u32[]{:S(2)}, u32[]{:S(2)}) collective-permute-start(f32[400,128]{1,0:T(8,128)S(1)} %pack.11.refs_6_), channel_id=1, source_target_pairs={{0,12},{4,0},{8,4},{12,8},{1,13},{5,1},{9,5},{13,9},{2,14},{6,2},{... | collective-permute-start | bytes 614408 | tf_op jit(solution)/shard_map/ppermute | solution.py:375
  14.8 1.3 %expand.1 = f32[160,160]{1,0:T(8,128)S(1)} custom-call(f32[1,81,81]{2,1,0:T(8,128)} %copy.20.half), custom_call_target="tpu_custom_call" | custom-call | bytes 1400 | tf_op jit(solution)/shard_map/expand/pallas_call | solution.py:459
  16.2 2.6 %place.1 = (s32[144]{0:T(256)S(1)}, s32[1]{0:T(128)}) custom-call(s32[144]{0:T(256)} %get-tuple-element.444.known, s32[128]{0:T(128)} %get-tuple-element.445.refs_0_, s32[128]{0:T(128)S(1)} %collective-permute-done.105.wanted.refs_1_.refs_0_, s32[128]{0:T(128)S(1)} %collective-permute-done.106.wanted.refs_2_.refs_1_, ...), custom_call_target="tpu_custom_call" | custom-call | bytes 2800 | tf_op jit(solution)/shard_map/place/pallas_call | solution.py:437
  25.8 4.5 %collective-permute-done.111 = f32[400,128]{1,0:T(8,128)} collective-permute-done((f32[400,128]{1,0:T(8,128)S(1)}, f32[400,128]{1,0:T(8,128)}, u32[]{:S(2)}, u32[]{:S(2)}) %collective-permute-start.111) | collective-permute-done | bytes 204832 | tf_op jit(solution)/shard_map/ppermute | solution.py:375
  30.4 49.0 %conditional.1 = (f32[64,1,6400]{2,1,0:T(1,128)S(1)}) conditional(s32[]{:T(128)} %bitcast.6, (f32[450,128]{1,0:T(8,128)S(1)}, f32[450,128]{1,0:T(8,128)S(1)}, f32[450,128]{1,0:T(8,128)S(1)}, s32[144]{0:T(256)S(1)}, f32[1200,128]{1,0:T(8,128)S(1)}, /*index=5*/f32[400,128]{1,0:T(8,128)}, f32[400,128]{1,0:T(8,128)}, ...), branch_computations={%region_0.0_spmd, %region_1.0_spmd, %region_2.0_spmd, %region_3.0_... | conditional | bytes 22132148 | solution.py:499
  30.4 1.4 %density.15 = (f32[300,128]{1,0:T(8,128)S(1)}, f32[300,128]{1,0:T(8,128)S(1)}, f32[300,128]{1,0:T(8,128)S(1)}, f32[300,128]{1,0:T(8,128)S(1)}, f32[1200,128]{1,0:T(8,128)S(1)}) custom-call(s32[144]{0:T(256)S(1)} %get-tuple-element.196.place, f32[1200,128]{1,0:T(8,128)S(1)} %get-tuple-element.206.owned, f32[400,128]{1,0:T(8,128)} %get-tuple-element.200.refs_0_, ...), custom_call_target="tpu_custom_call" | custom-call | bytes 1200 | tf_op jit(solution)/shard_map/cond/branch_0_fun/density/pallas_call | solution.py:379
  34.3 1.5 %collective-permute-start.2 = (f32[450,128]{1,0:T(8,128)S(1)}, f32[450,128]{1,0:T(8,128)S(1)}, u32[]{:S(2)}, u32[]{:S(2)}) collective-permute-start(f32[450,128]{1,0:T(8,128)S(1)} %get-tuple-element.205), channel_id=1, source_target_pairs={{0,12},{4,0},{8,4},{12,8},{1,13},{5,1},{9,5},{13,9},{2,14},{6,2},{... | collective-permute-start | bytes 691208 | tf_op jit(solution)/shard_map/cond/branch_0_fun/ppermute | solution.py:476
  35.8 2.1 %collective-permute-done.4.refs_2_ = f32[300,128]{1,0:T(8,128)S(1)} collective-permute-done((f32[300,128]{1,0:T(8,128)S(1)}, f32[300,128]{1,0:T(8,128)S(1)}, u32[]{:S(2)}, u32[]{:S(2)}) %collective-permute-start.4) | collective-permute-done | bytes 153632 | tf_op jit(solution)/shard_map/cond/branch_0_fun/ppermute | solution.py:327
  37.9 3.8 %collective-permute-done.5.refs_3_ = f32[300,128]{1,0:T(8,128)S(1)} collective-permute-done((f32[300,128]{1,0:T(8,128)S(1)}, f32[300,128]{1,0:T(8,128)S(1)}, u32[]{:S(2)}, u32[]{:S(2)}) %collective-permute-start.5) | collective-permute-done | bytes 153632 | tf_op jit(solution)/shard_map/cond/branch_0_fun/ppermute | solution.py:327
  41.7 2.7 %transform.15 = (f32[300,128]{1,0:T(8,128)S(1)}, f32[300,128]{1,0:T(8,128)S(1)}, f32[300,128]{1,0:T(8,128)S(1)}, f32[300,128]{1,0:T(8,128)S(1)}) custom-call(f32[300,128]{1,0:T(8,128)S(1)} %get-tuple-element.207.refs_0_, f32[300,128]{1,0:T(8,128)S(1)} %collective-permute-done.3.refs_1_, f32[300,128]{1,0:T(8,128)S(1)} %collective-permute-done.4.refs_2_, ...), custom_call_target="tpu_custom_call" | custom-call | bytes 2900 | tf_op jit(solution)/shard_map/cond/branch_0_fun/transform/pallas_call | solution.py:391
  46.1 8.1 %collective-permute-done.1.refs_4_ = f32[450,128]{1,0:T(8,128)S(1)} collective-permute-done((f32[450,128]{1,0:T(8,128)S(1)}, f32[450,128]{1,0:T(8,128)S(1)}, u32[]{:S(2)}, u32[]{:S(2)}) %collective-permute-start.1) | collective-permute-done | bytes 230432 | tf_op jit(solution)/shard_map/cond/branch_0_fun/ppermute | solution.py:476
  54.2 1.3 %collective-permute-done.2.refs_5_ = f32[450,128]{1,0:T(8,128)S(1)} collective-permute-done((f32[450,128]{1,0:T(8,128)S(1)}, f32[450,128]{1,0:T(8,128)S(1)}, u32[]{:S(2)}, u32[]{:S(2)}) %collective-permute-start.2) | collective-permute-done | bytes 230432 | tf_op jit(solution)/shard_map/cond/branch_0_fun/ppermute | solution.py:476
  55.5 1.3 %density.17 = (f32[150,128]{1,0:T(8,128)S(1)}, f32[150,128]{1,0:T(8,128)S(1)}, f32[150,128]{1,0:T(8,128)S(1)}, f32[150,128]{1,0:T(8,128)S(1)}, f32[600,128]{1,0:T(8,128)S(1)}) custom-call(s32[144]{0:T(256)S(1)} %get-tuple-element.196.place, f32[600,128]{1,0:T(8,128)S(1)} %get-tuple-element.231.owned, f32[400,128]{1,0:T(8,128)} %get-tuple-element.200.refs_0_, ...), custom_call_target="tpu_custom_call" | custom-call | bytes 600 | tf_op jit(solution)/shard_map/cond/branch_0_fun/density/pallas_call | solution.py:379
  62.3 1.5 %collective-permute-start.10 = (f32[150,128]{1,0:T(8,128)S(1)}, f32[150,128]{1,0:T(8,128)S(1)}, u32[]{:S(2)}, u32[]{:S(2)}) collective-permute-start(f32[150,128]{1,0:T(8,128)S(1)} %get-tuple-element.226), channel_id=1, source_target_pairs={{0,3},{1,2},{2,1},{3,0},{4,7},{5,6},{6,5},{7,4},{8,11},{9,10},{10,... | collective-permute-start | bytes 230408 | tf_op jit(solution)/shard_map/cond/branch_0_fun/ppermute | solution.py:327
  63.8 1.5 %transform.17 = (f32[150,128]{1,0:T(8,128)S(1)}, f32[150,128]{1,0:T(8,128)S(1)}, f32[150,128]{1,0:T(8,128)S(1)}, f32[150,128]{1,0:T(8,128)S(1)}) custom-call(f32[150,128]{1,0:T(8,128)S(1)} %get-tuple-element.233.refs_0_, f32[150,128]{1,0:T(8,128)S(1)} %collective-permute-done.14.refs_1_, f32[150,128]{1,0:T(8,128)S(1)} %collective-permute-done.15.refs_2_, ...), custom_call_target="tpu_custom_call" | custom-call | bytes 1700 | tf_op jit(solution)/shard_map/cond/branch_0_fun/transform/pallas_call | solution.py:391
  65.4 1.6 %collective-permute-done.10.refs_3_ = f32[150,128]{1,0:T(8,128)S(1)} collective-permute-done((f32[150,128]{1,0:T(8,128)S(1)}, f32[150,128]{1,0:T(8,128)S(1)}, u32[]{:S(2)}, u32[]{:S(2)}) %collective-permute-start.10) | collective-permute-done | bytes 76832 | tf_op jit(solution)/shard_map/cond/branch_0_fun/ppermute | solution.py:327
  67.0 1.5 %transform.16 = (f32[150,128]{1,0:T(8,128)S(1)}, f32[150,128]{1,0:T(8,128)S(1)}, f32[150,128]{1,0:T(8,128)S(1)}, f32[150,128]{1,0:T(8,128)S(1)}) custom-call(f32[150,128]{1,0:T(8,128)S(1)} %get-tuple-element.223.refs_0_, f32[150,128]{1,0:T(8,128)S(1)} %collective-permute-done.8.refs_1_, f32[150,128]{1,0:T(8,128)S(1)} %collective-permute-done.9.refs_2_, ...), custom_call_target="tpu_custom_call" | custom-call | bytes 1700 | tf_op jit(solution)/shard_map/cond/branch_0_fun/transform/pallas_call | solution.py:391
  73.4 1.6 %collective-permute-done.19.refs_4_ = f32[150,128]{1,0:T(8,128)S(1)} collective-permute-done((f32[150,128]{1,0:T(8,128)S(1)}, f32[150,128]{1,0:T(8,128)S(1)}, u32[]{:S(2)}, u32[]{:S(2)}) %collective-permute-start.19) | collective-permute-done | bytes 76832 | tf_op jit(solution)/shard_map/cond/branch_0_fun/ppermute | solution.py:327
  76.4 1.7 %collective-permute-done.13.refs_4_ = f32[150,128]{1,0:T(8,128)S(1)} collective-permute-done((f32[150,128]{1,0:T(8,128)S(1)}, f32[150,128]{1,0:T(8,128)S(1)}, u32[]{:S(2)}, u32[]{:S(2)}) %collective-permute-start.13) | collective-permute-done | bytes 76832 | tf_op jit(solution)/shard_map/cond/branch_0_fun/ppermute | solution.py:327
  (89 shorter events, 25.4 us)
Async XLA Ops:
  3.1 4.7 %collective-permute-start.105 = (s32[128]{0:T(128)}, s32[128]{0:T(128)S(1)}, u32[]{:S(2)}, u32[]{:S(2)}) collective-permute-start(s32[128]{0:T(128)} %get-tuple-element.445.refs_0_), channel_id=1, source_target_pairs={{0,12},{4,0},{8,4},{12,8},{1,13},{5,1},{9,5},{13,9},{2,14},{6,2},{... | collective-permute-start | bytes 1544 | tf_op jit(solution)/shard_map/ppermute | solution.py:360
  3.2 6.2 %collective-permute-start.106 = (s32[128]{0:T(128)}, s32[128]{0:T(128)S(1)}, u32[]{:S(2)}, u32[]{:S(2)}) collective-permute-start(s32[128]{0:T(128)} %get-tuple-element.446), channel_id=1, source_target_pairs={{0,8},{4,12},{8,0},{12,4},{1,9},{5,13},{9,1},{13,5},{2,10},{6,14},... | collective-permute-start | bytes 1544 | tf_op jit(solution)/shard_map/ppermute | solution.py:360
  5.7 6.5 %collective-permute-start.107 = (s32[128]{0:T(128)}, s32[128]{0:T(128)S(1)}, u32[]{:S(2)}, u32[]{:S(2)}) collective-permute-start(s32[128]{0:T(128)} %get-tuple-element.447), channel_id=1, source_target_pairs={{0,4},{4,8},{8,12},{12,0},{1,5},{5,9},{9,13},{13,1},{2,6},{6,10},{... | collective-permute-start | bytes 1544 | tf_op jit(solution)/shard_map/ppermute | solution.py:360
  9.4 15.5 %collective-permute-start.109 = (f32[400,128]{1,0:T(8,128)S(1)}, f32[400,128]{1,0:T(8,128)}, u32[]{:S(2)}, u32[]{:S(2)}) collective-permute-start(f32[400,128]{1,0:T(8,128)S(1)} %pack.9.refs_4_), channel_id=1, source_target_pairs={{0,4},{4,8},{8,12},{12,0},{1,5},{5,9},{9,13},{13,1},{2,6},{6,10},{... | collective-permute-start | bytes 614408 | tf_op jit(solution)/shard_map/ppermute | solution.py:375
  10.0 15.8 %collective-permute-start.110 = (f32[400,128]{1,0:T(8,128)S(1)}, f32[400,128]{1,0:T(8,128)}, u32[]{:S(2)}, u32[]{:S(2)}) collective-permute-start(f32[400,128]{1,0:T(8,128)S(1)} %pack.10.refs_5_), channel_id=1, source_target_pairs={{0,8},{4,12},{8,0},{12,4},{1,9},{5,13},{9,1},{13,5},{2,10},{6,14},... | collective-permute-start | bytes 614408 | tf_op jit(solution)/shard_map/ppermute | solution.py:375
  12.7 17.6 %collective-permute-start.111 = (f32[400,128]{1,0:T(8,128)S(1)}, f32[400,128]{1,0:T(8,128)}, u32[]{:S(2)}, u32[]{:S(2)}) collective-permute-start(f32[400,128]{1,0:T(8,128)S(1)} %pack.11.refs_6_), channel_id=1, source_target_pairs={{0,12},{4,0},{8,4},{12,8},{1,13},{5,1},{9,5},{13,9},{2,14},{6,2},{... | collective-permute-start | bytes 614408 | tf_op jit(solution)/shard_map/ppermute | solution.py:375
  32.3 5.6 %collective-permute-start.4 = (f32[300,128]{1,0:T(8,128)S(1)}, f32[300,128]{1,0:T(8,128)S(1)}, u32[]{:S(2)}, u32[]{:S(2)}) collective-permute-start(f32[300,128]{1,0:T(8,128)S(1)} %get-tuple-element.209), channel_id=1, source_target_pairs={{0,2},{1,3},{2,0},{3,1},{4,6},{5,7},{6,4},{7,5},{8,10},{9,11},{10,... | collective-permute-start | bytes 460808 | tf_op jit(solution)/shard_map/cond/branch_0_fun/ppermute | solution.py:327
  33.5 8.2 %collective-permute-start.5 = (f32[300,128]{1,0:T(8,128)S(1)}, f32[300,128]{1,0:T(8,128)S(1)}, u32[]{:S(2)}, u32[]{:S(2)}) collective-permute-start(f32[300,128]{1,0:T(8,128)S(1)} %get-tuple-element.210), channel_id=1, source_target_pairs={{0,3},{1,2},{2,1},{3,0},{4,7},{5,6},{6,5},{7,4},{8,11},{9,10},{10,... | collective-permute-start | bytes 460808 | tf_op jit(solution)/shard_map/cond/branch_0_fun/ppermute | solution.py:327
  34.0 12.0 %collective-permute-start = (f32[450,128]{1,0:T(8,128)S(1)}, f32[450,128]{1,0:T(8,128)S(1)}, u32[]{:S(2)}, u32[]{:S(2)}) collective-permute-start(f32[450,128]{1,0:T(8,128)S(1)} %get-tuple-element.203), channel_id=1, source_target_pairs={{0,4},{4,8},{8,12},{12,0},{1,5},{5,9},{9,13},{13,1},{2,6},{6,10},{... | collective-permute-start | bytes 691208 | tf_op jit(solution)/shard_map/cond/branch_0_fun/ppermute | solution.py:476
  34.0 20.2 %collective-permute-start.1 = (f32[450,128]{1,0:T(8,128)S(1)}, f32[450,128]{1,0:T(8,128)S(1)}, u32[]{:S(2)}, u32[]{:S(2)}) collective-permute-start(f32[450,128]{1,0:T(8,128)S(1)} %get-tuple-element.204), channel_id=1, source_target_pairs={{0,8},{4,12},{8,0},{12,4},{1,9},{5,13},{9,1},{13,5},{2,10},{6,14},... | collective-permute-start | bytes 691208 | tf_op jit(solution)/shard_map/cond/branch_0_fun/ppermute | solution.py:476
  34.3 21.2 %collective-permute-start.2 = (f32[450,128]{1,0:T(8,128)S(1)}, f32[450,128]{1,0:T(8,128)S(1)}, u32[]{:S(2)}, u32[]{:S(2)}) collective-permute-start(f32[450,128]{1,0:T(8,128)S(1)} %get-tuple-element.205), channel_id=1, source_target_pairs={{0,12},{4,0},{8,4},{12,8},{1,13},{5,1},{9,5},{13,9},{2,14},{6,2},{... | collective-permute-start | bytes 691208 | tf_op jit(solution)/shard_map/cond/branch_0_fun/ppermute | solution.py:476
  44.4 11.1 %collective-permute-start.6 = (f32[300,128]{1,0:T(8,128)S(1)}, f32[300,128]{1,0:T(8,128)S(1)}, u32[]{:S(2)}, u32[]{:S(2)}) collective-permute-start(f32[300,128]{1,0:T(8,128)S(1)} %get-tuple-element.220), channel_id=1, source_target_pairs={{0,2},{1,3},{2,0},{3,1},{4,6},{5,7},{6,4},{7,5},{8,10},{9,11},{10,... | collective-permute-start | bytes 460808 | tf_op jit(solution)/shard_map/cond/branch_0_fun/ppermute | solution.py:327
  45.7 9.8 %collective-permute-start.7 = (f32[300,128]{1,0:T(8,128)S(1)}, f32[300,128]{1,0:T(8,128)S(1)}, u32[]{:S(2)}, u32[]{:S(2)}) collective-permute-start(f32[300,128]{1,0:T(8,128)S(1)} %get-tuple-element.221), channel_id=1, source_target_pairs={{0,3},{1,2},{2,1},{3,0},{4,7},{5,6},{6,5},{7,4},{8,11},{9,10},{10,... | collective-permute-start | bytes 460808 | tf_op jit(solution)/shard_map/cond/branch_0_fun/ppermute | solution.py:327
  57.4 4.8 %collective-permute-start.15 = (f32[150,128]{1,0:T(8,128)S(1)}, f32[150,128]{1,0:T(8,128)S(1)}, u32[]{:S(2)}, u32[]{:S(2)}) collective-permute-start(f32[150,128]{1,0:T(8,128)S(1)} %get-tuple-element.235), channel_id=1, source_target_pairs={{0,2},{1,3},{2,0},{3,1},{4,6},{5,7},{6,4},{7,5},{8,10},{9,11},{10,... | collective-permute-start | bytes 230408 | tf_op jit(solution)/shard_map/cond/branch_0_fun/ppermute | solution.py:327
  58.7 5.1 %collective-permute-start.16 = (f32[150,128]{1,0:T(8,128)S(1)}, f32[150,128]{1,0:T(8,128)S(1)}, u32[]{:S(2)}, u32[]{:S(2)}) collective-permute-start(f32[150,128]{1,0:T(8,128)S(1)} %get-tuple-element.236), channel_id=1, source_target_pairs={{0,3},{1,2},{2,1},{3,0},{4,7},{5,6},{6,5},{7,4},{8,11},{9,10},{10,... | collective-permute-start | bytes 230408 | tf_op jit(solution)/shard_map/cond/branch_0_fun/ppermute | solution.py:327
  59.2 11.5 %collective-permute-start.20 = (f32[300,128]{1,0:T(8,128)S(1)}, f32[300,128]{1,0:T(8,128)S(1)}, u32[]{:S(2)}, u32[]{:S(2)}) collective-permute-start(f32[300,128]{1,0:T(8,128)S(1)} %get-tuple-element.243), channel_id=1, source_target_pairs={{0,1},{1,0},{2,3},{3,2},{4,5},{5,4},{6,7},{7,6},{8,9},{9,8},{10,11... | collective-permute-start | bytes 460808 | tf_op jit(solution)/shard_map/cond/branch_0_fun/ppermute | solution.py:327
  60.7 4.7 %collective-permute-start.8 = (f32[150,128]{1,0:T(8,128)S(1)}, f32[150,128]{1,0:T(8,128)S(1)}, u32[]{:S(2)}, u32[]{:S(2)}) collective-permute-start(f32[150,128]{1,0:T(8,128)S(1)} %get-tuple-element.224), channel_id=1, source_target_pairs={{0,1},{1,0},{2,3},{3,2},{4,5},{5,4},{6,7},{7,6},{8,9},{9,8},{10,11... | collective-permute-start | bytes 230408 | tf_op jit(solution)/shard_map/cond/branch_0_fun/ppermute | solution.py:327
  62.3 4.7 %collective-permute-start.10 = (f32[150,128]{1,0:T(8,128)S(1)}, f32[150,128]{1,0:T(8,128)S(1)}, u32[]{:S(2)}, u32[]{:S(2)}) collective-permute-start(f32[150,128]{1,0:T(8,128)S(1)} %get-tuple-element.226), channel_id=1, source_target_pairs={{0,3},{1,2},{2,1},{3,0},{4,7},{5,6},{6,5},{7,4},{8,11},{9,10},{10,... | collective-permute-start | bytes 230408 | tf_op jit(solution)/shard_map/cond/branch_0_fun/ppermute | solution.py:327
  65.3 6.6 %collective-permute-start.17 = (f32[150,128]{1,0:T(8,128)S(1)}, f32[150,128]{1,0:T(8,128)S(1)}, u32[]{:S(2)}, u32[]{:S(2)}) collective-permute-start(f32[150,128]{1,0:T(8,128)S(1)} %get-tuple-element.238), channel_id=1, source_target_pairs={{0,1},{1,0},{2,3},{3,2},{4,5},{5,4},{6,7},{7,6},{8,9},{9,8},{10,11... | collective-permute-start | bytes 230408 | tf_op jit(solution)/shard_map/cond/branch_0_fun/ppermute | solution.py:327
  68.5 7.3 %collective-permute-start.11 = (f32[150,128]{1,0:T(8,128)S(1)}, f32[150,128]{1,0:T(8,128)S(1)}, u32[]{:S(2)}, u32[]{:S(2)}) collective-permute-start(f32[150,128]{1,0:T(8,128)S(1)} %get-tuple-element.228), channel_id=1, source_target_pairs={{0,1},{1,0},{2,3},{3,2},{4,5},{5,4},{6,7},{7,6},{8,9},{9,8},{10,11... | collective-permute-start | bytes 230408 | tf_op jit(solution)/shard_map/cond/branch_0_fun/ppermute | solution.py:327
  68.9 4.5 %collective-permute-start.18 = (f32[150,128]{1,0:T(8,128)S(1)}, f32[150,128]{1,0:T(8,128)S(1)}, u32[]{:S(2)}, u32[]{:S(2)}) collective-permute-start(f32[150,128]{1,0:T(8,128)S(1)} %get-tuple-element.239), channel_id=1, source_target_pairs={{0,2},{1,3},{2,0},{3,1},{4,6},{5,7},{6,4},{7,5},{8,10},{9,11},{10,... | collective-permute-start | bytes 230408 | tf_op jit(solution)/shard_map/cond/branch_0_fun/ppermute | solution.py:327
  70.1 4.9 %collective-permute-start.19 = (f32[150,128]{1,0:T(8,128)S(1)}, f32[150,128]{1,0:T(8,128)S(1)}, u32[]{:S(2)}, u32[]{:S(2)}) collective-permute-start(f32[150,128]{1,0:T(8,128)S(1)} %get-tuple-element.240), channel_id=1, source_target_pairs={{0,3},{1,2},{2,1},{3,0},{4,7},{5,6},{6,5},{7,4},{8,11},{9,10},{10,... | collective-permute-start | bytes 230408 | tf_op jit(solution)/shard_map/cond/branch_0_fun/ppermute | solution.py:327
  70.7 5.7 %collective-permute-start.12 = (f32[150,128]{1,0:T(8,128)S(1)}, f32[150,128]{1,0:T(8,128)S(1)}, u32[]{:S(2)}, u32[]{:S(2)}) collective-permute-start(f32[150,128]{1,0:T(8,128)S(1)} %get-tuple-element.229), channel_id=1, source_target_pairs={{0,2},{1,3},{2,0},{3,1},{4,6},{5,7},{6,4},{7,5},{8,10},{9,11},{10,... | collective-permute-start | bytes 230408 | tf_op jit(solution)/shard_map/cond/branch_0_fun/ppermute | solution.py:327
  71.9 6.2 %collective-permute-start.13 = (f32[150,128]{1,0:T(8,128)S(1)}, f32[150,128]{1,0:T(8,128)S(1)}, u32[]{:S(2)}, u32[]{:S(2)}) collective-permute-start(f32[150,128]{1,0:T(8,128)S(1)} %get-tuple-element.230), channel_id=1, source_target_pairs={{0,3},{1,2},{2,1},{3,0},{4,7},{5,6},{6,5},{7,4},{8,11},{9,10},{10,... | collective-permute-start | bytes 230408 | tf_op jit(solution)/shard_map/cond/branch_0_fun/ppermute | solution.py:327
  (22 other events, 151.4 us)
